TPU v7x, 128 devices: a whole 4x4x4 slice. The times are simulated.
128 devices in a mesh: dp: 4 (over y), context: 8 (over z, x_hi), tensor: 4 (over x_lo, core).
Axes of the slice: x: 4 (x_hi: 2, x_lo: 2; x = x_hi * 2 + x_lo), y: 4, z: 4, core: 2. Of those that a mesh axis runs over, the one named last changes fastest.
Arguments:
- tokens: bfloat16 [8, 1024, 2048], P('dp', 'context'), may hold values from -6 to 6
- attn_gain: bfloat16 [2048], replicated, may hold values from 0.5 to 1.5
- w_query: bfloat16 [2048, 2048], P(None, 'tensor'), may hold values from -0.125 to 0.125
- w_key: bfloat16 [2048, 1024], P(None, 'tensor'), may hold values from -0.125 to 0.125
- w_value: bfloat16 [2048, 1024], P(None, 'tensor'), may hold values from -0.125 to 0.125
- query_gain: bfloat16 [128], replicated, may hold values from 0.25 to 1.75
- key_gain: bfloat16 [128], replicated, may hold values from 0.25 to 1.75
- w_out: bfloat16 [2048, 2048], P('tensor'), may hold values from -1.5 to 1.5
- mlp_gain: bfloat16 [2048], replicated, may hold values from 0.5 to 1.5
- w_gate: bfloat16 [2048, 6144], P(None, 'tensor'), may hold values from -0.125 to 0.125
- w_up: bfloat16 [2048, 6144], P(None, 'tensor'), may hold values from -0.125 to 0.125
- w_down: bfloat16 [6144, 2048], P('tensor'), may hold values from -0.078125 to 0.078125
- out_grad: bfloat16 [8, 1024, 2048], P('dp', 'context'), may hold values from -6 to 6
Outputs:
- block_out: bfloat16 [8, 1024, 2048], P('dp', 'context')
- tokens_grad: bfloat16 [8, 1024, 2048], P('dp', 'context')
- attn_gain_grad: float32 [2048], replicated
- w_query_grad: float32 [2048, 2048], P(('dp', 'context'), 'tensor')
- w_key_grad: float32 [2048, 1024], P(('dp', 'context'), 'tensor')
- w_value_grad: float32 [2048, 1024], P(('dp', 'context'), 'tensor')
- query_gain_grad: float32 [128], replicated
- key_gain_grad: float32 [128], replicated
- w_out_grad: float32 [2048, 2048], P('tensor', ('dp', 'context'))
- mlp_gain_grad: float32 [2048], replicated
- w_gate_grad: float32 [2048, 6144], P(('dp', 'context'), 'tensor')
- w_up_grad: float32 [2048, 6144], P(('dp', 'context'), 'tensor')
- w_down_grad: float32 [6144, 2048], P('tensor', ('dp', 'context'))
All inputs are finite; a program needn't handle non-finite values.
Results may differ from a plain program's by a relative error of at most 0.029.
Values may be sent and summed in bfloat16 or wider, within the bound.
A program may use at most 256 MiB of HBM per device.

v0:
```python
import jax
import jax.numpy as jnp
from jax import lax
from jax.sharding import PartitionSpec as P

EPSILON = 1e-06
ROPE_BASE = 1000000.0


def matmul(left_op, right_op):
    return jnp.dot(left_op, right_op, preferred_element_type=jnp.float32)


def matmul_tn(left_op, right_op):
    return lax.dot_general(
        left_op, right_op, (((0,), (0,)), ((), ())), preferred_element_type=jnp.float32
    )


def matmul_nt(left_op, right_op):
    return lax.dot_general(
        left_op, right_op, (((1,), (1,)), ((), ())), preferred_element_type=jnp.float32
    )


def rms_scale(values):
    return lax.rsqrt(jnp.mean(values * values, axis=-1, keepdims=True) + EPSILON)


def rms_back(grad_normed, normed, inverse):
    return inverse * (grad_normed - normed * jnp.mean(grad_normed * normed, axis=-1, keepdims=True))


def rope_tables(first_place, length, head_dim):
    places = (first_place + jnp.arange(length, dtype=jnp.int32)).astype(jnp.float32)
    frequency = ROPE_BASE ** (-jnp.arange(0, head_dim, 2).astype(jnp.float32) / head_dim)
    angles = places[:, None] * frequency[None, :]
    return (jnp.cos(angles), jnp.sin(angles))


def rotate(values, cosine, sine_table):
    halfway = values.shape[-1] // 2
    front_part = values[..., :halfway]
    back_part = values[..., halfway:]
    cosine = cosine[:, None, :]
    sine_table = sine_table[:, None, :]
    return jnp.concatenate(
        [
            front_part * cosine - back_part * sine_table,
            back_part * cosine + front_part * sine_table,
        ],
        axis=-1,
    )


def local(
    tokens,
    attn_gain,
    w_query,
    w_key,
    w_value,
    query_gain,
    key_gain,
    w_out,
    mlp_gain,
    w_gate,
    w_up,
    w_down,
    out_grad,
):
    sequences, local_len, model_width = tokens.shape
    head_dim = query_gain.shape[0]
    kv_local = w_key.shape[1] // head_dim
    group_size = w_query.shape[1] // head_dim // kv_local
    row_count = sequences * local_len
    length = local_len * lax.axis_size("context")
    first_place = lax.axis_index("context") * local_len
    quarter = row_count // lax.axis_size("tensor")
    quarter_start = lax.axis_index("tensor") * quarter
    score_scale = head_dim ** (-0.5)
    inputs = tokens.reshape(row_count, model_width).astype(jnp.float32)
    gain_one = attn_gain.astype(jnp.float32)
    gain_two = mlp_gain.astype(jnp.float32)
    gain_query = query_gain.astype(jnp.float32)
    gain_key = key_gain.astype(jnp.float32)
    inverse_one = rms_scale(inputs)
    normed_one = inputs * inverse_one
    normed_one_b = (normed_one * gain_one).astype(jnp.bfloat16)
    query_proj = matmul(normed_one_b, w_query).reshape(row_count, kv_local * group_size, head_dim)
    key_proj = matmul(normed_one_b, w_key).reshape(row_count, kv_local, head_dim)
    value_rows = matmul(normed_one_b, w_value).astype(jnp.bfloat16)
    cosine, sine_table = rope_tables(first_place, local_len, head_dim)
    cos_rows = jnp.tile(cosine, (sequences, 1))
    sin_rows = jnp.tile(sine_table, (sequences, 1))
    inverse_query = rms_scale(query_proj)
    query_hat = query_proj * inverse_query
    query_rot = rotate(query_hat * gain_query, cos_rows, sin_rows).astype(jnp.bfloat16)
    inverse_key = rms_scale(key_proj)
    key_hat = key_proj * inverse_key
    key_rot = rotate(key_hat * gain_key, cos_rows, sin_rows).astype(jnp.bfloat16)
    grouped = query_rot.reshape(sequences, local_len, kv_local, group_size, head_dim)
    key_local = key_rot.reshape(sequences, local_len, kv_local * head_dim)
    value_local = value_rows.reshape(sequences, local_len, kv_local * head_dim)
    key_full, value_full = (
        lax.all_gather(key_local, "context", axis=1, tiled=True),
        lax.all_gather(value_local, "context", axis=1, tiled=True),
    )
    key_heads = key_full.reshape(sequences, length, kv_local, head_dim)
    value_heads = value_full.reshape(sequences, length, kv_local, head_dim)
    query_places = first_place + jnp.arange(local_len, dtype=jnp.int32)
    key_places = jnp.arange(length, dtype=jnp.int32)
    allowed = query_places[:, None] >= key_places[None, :]
    scores = (
        jnp.einsum("sikgd,sjkd->skgij", grouped, key_heads, preferred_element_type=jnp.float32)
        * score_scale
    )
    masked = jnp.where(allowed, scores, -1e30)
    row_max = jnp.max(masked, axis=-1, keepdims=True)
    exponent = jnp.exp(masked - row_max)
    totals = jnp.sum(exponent, axis=-1, keepdims=True)
    log_total = row_max + jnp.log(totals)
    probability_b = (exponent / totals).astype(jnp.bfloat16)
    mixture = jnp.einsum(
        "skgij,sjkd->sikgd", probability_b, value_heads, preferred_element_type=jnp.float32
    )
    mixture = mixture.reshape(row_count, kv_local * group_size * head_dim).astype(jnp.bfloat16)
    attention_out = lax.psum(matmul(mixture, w_out), "tensor")
    middle = inputs + attention_out
    inverse_two = rms_scale(middle)
    normed_two = middle * inverse_two
    normed_two_b = (normed_two * gain_two).astype(jnp.bfloat16)
    gate_rows = matmul(normed_two_b, w_gate)
    up_rows = matmul(normed_two_b, w_up)
    sigmoid_gate = jax.nn.sigmoid(gate_rows)
    silu_gate = gate_rows * sigmoid_gate
    hidden = (silu_gate * up_rows).astype(jnp.bfloat16)
    feed_out = lax.psum(matmul(hidden, w_down).astype(jnp.bfloat16), "tensor").astype(jnp.float32)
    block_out = (middle + feed_out).astype(jnp.bfloat16).reshape(sequences, local_len, model_width)
    grad_rows = out_grad.reshape(row_count, model_width)
    grad_hidden = matmul_nt(grad_rows, w_down)
    down_grad = matmul_tn(grad_rows, hidden)
    grad_gate = (
        grad_hidden * up_rows * sigmoid_gate * (1.0 + gate_rows * (1.0 - sigmoid_gate))
    ).astype(jnp.bfloat16)
    grad_up = (grad_hidden * silu_gate).astype(jnp.bfloat16)
    gate_grad = matmul_tn(normed_two_b, grad_gate)
    up_grad = matmul_tn(normed_two_b, grad_up)
    grad_normed_two = lax.psum(
        (matmul_nt(grad_gate, w_gate) + matmul_nt(grad_up, w_up)).astype(jnp.bfloat16), "tensor"
    ).astype(jnp.float32)
    gain_two_term = jnp.sum(
        lax.dynamic_slice_in_dim(grad_normed_two * normed_two, quarter_start, quarter, 0), axis=0
    )
    grad_middle = grad_rows.astype(jnp.float32) + rms_back(
        grad_normed_two * gain_two, normed_two, inverse_two
    )
    grad_branch = grad_middle.astype(jnp.bfloat16)
    out_weight_grad = matmul_tn(grad_branch, mixture)
    grad_mixture = matmul_nt(grad_branch, w_out).astype(jnp.bfloat16)
    grad_mixture = grad_mixture.reshape(sequences, local_len, kv_local, group_size, head_dim)
    scores_again = (
        jnp.einsum("sikgd,sjkd->skgij", grouped, key_heads, preferred_element_type=jnp.float32)
        * score_scale
    )
    probability = jnp.exp(jnp.where(allowed, scores_again, -1e30) - log_total)
    grad_prob = jnp.einsum(
        "sikgd,sjkd->skgij", grad_mixture, value_heads, preferred_element_type=jnp.float32
    )
    inner_sum = jnp.sum(probability * grad_prob, axis=-1, keepdims=True)
    grad_scores = (probability * (grad_prob - inner_sum)).astype(jnp.bfloat16)
    grad_query = (
        jnp.einsum("skgij,sjkd->sikgd", grad_scores, key_heads, preferred_element_type=jnp.float32)
        * score_scale
    )
    grad_key_full = (
        jnp.einsum("skgij,sikgd->sjkd", grad_scores, grouped, preferred_element_type=jnp.float32)
        * score_scale
    )
    grad_value_full = jnp.einsum(
        "skgij,sikgd->sjkd",
        probability.astype(jnp.bfloat16),
        grad_mixture,
        preferred_element_type=jnp.float32,
    )
    grad_key_own, grad_value_own = (
        lax.psum_scatter(
            grad_key_full.reshape(sequences, length, kv_local * head_dim).astype(jnp.bfloat16),
            "context",
            scatter_dimension=1,
            tiled=True,
        ).astype(jnp.float32),
        lax.psum_scatter(
            grad_value_full.reshape(sequences, length, kv_local * head_dim).astype(jnp.bfloat16),
            "context",
            scatter_dimension=1,
            tiled=True,
        ).astype(jnp.float32),
    )
    grad_query_normed = rotate(
        grad_query.reshape(row_count, kv_local * group_size, head_dim), cos_rows, -sin_rows
    )
    query_gain_term = jnp.sum(grad_query_normed * query_hat, axis=(0, 1))
    grad_query_proj = (
        rms_back(grad_query_normed * gain_query, query_hat, inverse_query)
        .reshape(row_count, -1)
        .astype(jnp.bfloat16)
    )
    grad_key_normed = rotate(
        grad_key_own.reshape(row_count, kv_local, head_dim), cos_rows, -sin_rows
    )
    key_gain_term = jnp.sum(grad_key_normed * key_hat, axis=(0, 1))
    grad_key_proj = (
        rms_back(grad_key_normed * gain_key, key_hat, inverse_key)
        .reshape(row_count, -1)
        .astype(jnp.bfloat16)
    )
    grad_value_b = grad_value_own.reshape(row_count, kv_local * head_dim).astype(jnp.bfloat16)
    grad_normed_one = lax.psum(
        (
            matmul_nt(grad_query_proj, w_query)
            + matmul_nt(grad_key_proj, w_key)
            + matmul_nt(grad_value_b, w_value)
        ).astype(jnp.bfloat16),
        "tensor",
    ).astype(jnp.float32)
    gain_one_term = jnp.sum(
        lax.dynamic_slice_in_dim(grad_normed_one * normed_one, quarter_start, quarter, 0), axis=0
    )
    tokens_grad = (
        grad_middle + rms_back(grad_normed_one * gain_one, normed_one, inverse_one)
    ).astype(jnp.bfloat16)
    tokens_grad = tokens_grad.reshape(sequences, local_len, model_width)
    query_grad = matmul_tn(normed_one_b, grad_query_proj)
    key_grad = matmul_tn(normed_one_b, grad_key_proj)
    value_grad = matmul_tn(normed_one_b, grad_value_b)
    gain_grads = lax.psum(
        (gain_one_term, query_gain_term, key_gain_term, gain_two_term), ("dp", "context", "tensor")
    )
    query_part, key_part, value_part, out_part, gate_part, up_part, down_part = (
        lax.psum_scatter(
            query_grad.astype(jnp.bfloat16), ("dp", "context"), scatter_dimension=0, tiled=True
        ).astype(jnp.float32),
        lax.psum_scatter(
            key_grad.astype(jnp.bfloat16), ("dp", "context"), scatter_dimension=0, tiled=True
        ).astype(jnp.float32),
        lax.psum_scatter(
            value_grad.astype(jnp.bfloat16), ("dp", "context"), scatter_dimension=0, tiled=True
        ).astype(jnp.float32),
        lax.psum_scatter(
            out_weight_grad.astype(jnp.bfloat16), ("dp", "context"), scatter_dimension=0, tiled=True
        ).astype(jnp.float32),
        lax.psum_scatter(
            gate_grad.astype(jnp.bfloat16), ("dp", "context"), scatter_dimension=0, tiled=True
        ).astype(jnp.float32),
        lax.psum_scatter(
            up_grad.astype(jnp.bfloat16), ("dp", "context"), scatter_dimension=0, tiled=True
        ).astype(jnp.float32),
        lax.psum_scatter(
            down_grad.astype(jnp.bfloat16), ("dp", "context"), scatter_dimension=0, tiled=True
        ).astype(jnp.float32),
    )
    return (
        block_out,
        tokens_grad,
        gain_grads[0],
        query_part,
        key_part,
        value_part,
        gain_grads[1],
        gain_grads[2],
        out_part.T,
        gain_grads[3],
        gate_part,
        up_part,
        down_part.T,
    )


def solution(mesh):
    in_specs = (
        P("dp", "context", None),
        P(),
        P(None, "tensor"),
        P(None, "tensor"),
        P(None, "tensor"),
        P(),
        P(),
        P("tensor", None),
        P(),
        P(None, "tensor"),
        P(None, "tensor"),
        P("tensor", None),
        P("dp", "context", None),
    )
    out_specs = (
        P("dp", "context", None),
        P("dp", "context", None),
        P(),
        P(("dp", "context"), "tensor"),
        P(("dp", "context"), "tensor"),
        P(("dp", "context"), "tensor"),
        P(),
        P(),
        P("tensor", ("dp", "context")),
        P(),
        P(("dp", "context"), "tensor"),
        P(("dp", "context"), "tensor"),
        P("tensor", ("dp", "context")),
    )
    return jax.shard_map(local, mesh=mesh, in_specs=in_specs, out_specs=out_specs, check_vma=False)
```

profile of v0, /device:TPU:0, one launch (start us, length us, event | category | flops | bytes accessed | tf_op | source)
XLA Modules:
  0.0 2028.2 jit_solution(11875871166141847826)
XLA Ops:
  10.9 2.3 copy.100
  16.6 1.6 convert_element_type.216
  18.2 1.6 copy.68
  19.9 1.7 bitcast_multiply_fusion.2
  22.8 4.0 copy.103
  26.7 2.7 multiply_reduce_fusion.5
  31.1 1.6 concatenate.20
  32.7 1.8 copy.70
  34.5 1.6 concatenate.21
  36.1 1.8 copy.71
  38.6 29.3 %all-gather.5.cloned.1.call-done = bf16[2,1024,256]{1,2,0:T(8,128)(2,1)} async-done(((bf16[2,128,256]{1,2,0:T(8,128)(2,1)}), bf16[2,1024,256]{1,2,0:T(8,128)(2,1)}) %all-gather.5.cloned.1.call-update) | async-done | bytes 1048592 | tf_op jit(solution)/shard_map/all_gather | solution.py:105
  67.9 2.4 fusion.33
  70.3 2.0 copy-done.2
  72.8 42.5 %all-gather.3.cloned.1.call-done = bf16[2,1024,256]{2,1,0:T(8,128)(2,1)} async-done(((bf16[2,128,256]{2,1,0:T(8,128)(2,1)}), bf16[2,1024,256]{2,1,0:T(8,128)(2,1)}) %all-gather.3.cloned.1.call-update) | async-done | bytes 1048592 | tf_op jit(solution)/shard_map/all_gather | solution.py:106
  115.4 2.3 copy.66
  117.6 4.1 fusion.23
  121.7 1.8 copy.74
  123.5 1.8 convert_element_type.221
  125.3 3.1 fusion.34
  129.0 55.6 %all-reduce.6.cloned.1.call-done = f32[256,2048]{1,0:T(8,128)} async-done(((f32[256,2048]{1,0:T(8,128)}), f32[256,2048]{1,0:T(8,128)}) %all-reduce.6.cloned.1.call-update) | async-done | bytes 2097168 | tf_op jit(solution)/shard_map/psum | solution.py:127
  184.6 2.1 multiply_reduce_fusion.2
  186.8 1.9 multiply_convert_fusion
  188.7 5.1 fusion.36
  193.9 1.8 fusion.35
  195.8 3.3 multiply_convert_fusion.2
  199.2 1.8 fusion.37
  201.0 2.9 fusion.8
  204.0 42.5 %all-reduce.8.cloned.1.call-done = bf16[256,2048]{1,0:T(8,128)(2,1)} async-done(((bf16[256,2048]{1,0:T(8,128)(2,1)}), bf16[256,2048]{1,0:T(8,128)(2,1)}) %all-reduce.8.cloned.1.call-update) | async-done | bytes 1048592 | tf_op jit(solution)/shard_map/psum | solution.py:148
  246.5 2.4 multiply_reduce_fusion.1
  249.3 1.8 multiply_add_fusion
  255.9 3.0 bitcast_convert_fusion
  260.6 3.5 fusion.1
  265.1 1.9 fusion.12
  267.1 49.6 %copy.108 = bf16[2,1024,256]{0,2,1:T(8,128)(2,1)} copy(bf16[2,1024,256]{1,2,0:T(8,128)(2,1)} %bitcast.166) | data formatting | bytes 2097152
  316.6 97.3 %reshape.315 = bf16[1024,512]{1,0:T(8,128)(2,1)} reshape(bf16[1024,256,2]{2,1,0:T(8,128)(2,1)} %bitcast.40) | data formatting | bytes 2097152
  414.9 5.9 convolution_convert_fusion.6
  420.7 1.7 fusion.21
  429.0 2.7 fusion.39
  431.7 55.2 %reduce-scatter.28.cloned.1.call-done = bf16[128,512]{1,0:T(8,128)(2,1)} async-done(((bf16[1024,512]{1,0:T(8,128)(2,1)}), bf16[128,512]{1,0:T(8,128)(2,1)}) %reduce-scatter.28.cloned.1.call-update) | async-done | bytes 131088
  486.9 19.9 reshape.316
  506.8 8.4 copy.109
  517.0 1.7 fusion.38
  518.7 1.8 fusion.7
  521.7 1.5 fusion.9
  523.3 2.2 convolution_convert_fusion.4
  525.6 2.8 convolution_convert_fusion.5
  528.5 2.1 convolution_convert_fusion.3
  532.0 4.5 fusion
  536.5 8.7 copy.110
  546.6 4.5 convolution_convert_fusion.1
  552.2 4.4 convolution_convert_fusion.2
  559.3 17.9 all-reduce.10.cloned.1.call-done
  577.2 3.0 convert_element_type.249
  580.2 186.4 %reduce-scatter.20.cloned.1.call-done = bf16[64,256]{1,0:T(8,128)(2,1)} async-done(((bf16[2048,256]{1,0:T(8,128)(2,1)}), bf16[64,256]{1,0:T(8,128)(2,1)}) %reduce-scatter.20.cloned.1.call-update) | async-done | bytes 32784 | tf_op jit(solution)/shard_map/reduce_scatter | solution.py:246
  768.0 184.0 %reduce-scatter.16.cloned.1.call-done = bf16[64,512]{1,0:T(8,128)(2,1)} async-done(((bf16[2048,512]{1,0:T(8,128)(2,1)}), bf16[64,512]{1,0:T(8,128)(2,1)}) %reduce-scatter.16.cloned.1.call-update) | async-done | bytes 65552 | tf_op jit(solution)/shard_map/reduce_scatter | solution.py:240
  953.4 181.5 %reduce-scatter.18.cloned.1.call-done = bf16[64,256]{1,0:T(8,128)(2,1)} async-done(((bf16[2048,256]{1,0:T(8,128)(2,1)}), bf16[64,256]{1,0:T(8,128)(2,1)}) %reduce-scatter.18.cloned.1.call-update) | async-done | bytes 32784 | tf_op jit(solution)/shard_map/reduce_scatter | solution.py:243
  1137.7 65.1 %all-reduce = (f32[2048]{0:T(1024)}, f32[128]{0:T(128)}, f32[128]{0:T(128)}, f32[2048]{0:T(1024)}) all-reduce(f32[2048]{0:T(1024)S(1)} %fusion.25, f32[128]{0:T(128)S(1)} %copy-done.46, f32[128]{0:T(128)S(1)} %copy-done.47, f32[2048]{0:T(1024)S(1)} %fusion.24), channel_id=1, replica_groups=mesh['dp'=4,'context'=8,'tensor'=4] {'dp','context','tensor'}, use_global_device_ids=true, to_apply=%region_18.19 | all-reduce | flops 4352 | bytes 34816 | tf_op jit(solution)/shard_map/psum | solution.py:236
  1203.3 117.4 %reduce-scatter.22.cloned.1.call-done = bf16[64,512]{1,0:T(8,128)(2,1)} async-done(((bf16[2048,512]{1,0:T(8,128)(2,1)}), bf16[64,512]{1,0:T(8,128)(2,1)}) %reduce-scatter.22.cloned.1.call-update) | async-done | bytes 65552 | tf_op jit(solution)/shard_map/reduce_scatter | solution.py:249
  1322.2 5.5 add_convert_fusion
  1327.7 224.2 %reduce-scatter.30.cloned.1.call-done = bf16[64,1536]{1,0:T(8,128)(2,1)} async-done(((bf16[2048,1536]{1,0:T(8,128)(2,1)}), bf16[64,1536]{1,0:T(8,128)(2,1)}) %reduce-scatter.30.cloned.1.call-update) | async-done | bytes 196624
  1554.1 231.7 %reduce-scatter.26.cloned.1.call-done = bf16[64,1536]{1,0:T(8,128)(2,1)} async-done(((bf16[2048,1536]{1,0:T(8,128)(2,1)}), bf16[64,1536]{1,0:T(8,128)(2,1)}) %reduce-scatter.26.cloned.1.call-update) | async-done | bytes 196624 | tf_op jit(solution)/shard_map/reduce_scatter | solution.py:255
  1785.8 1.7 convert_element_type.261
  1787.5 231.9 %reduce-scatter.24.cloned.1.call-done = bf16[64,1536]{1,0:T(8,128)(2,1)} async-done(((bf16[2048,1536]{1,0:T(8,128)(2,1)}), bf16[64,1536]{1,0:T(8,128)(2,1)}) %reduce-scatter.24.cloned.1.call-update) | async-done | bytes 196624 | tf_op jit(solution)/shard_map/reduce_scatter | solution.py:252
  2019.4 1.7 convert_element_type.259
  (198 shorter events, 47.0 us)
Async XLA Ops:
  7.2 118.1 %copy-start = (bf16[512,2048]{1,0:T(8,128)(2,1)S(1)}, bf16[512,2048]{1,0:T(8,128)(2,1)}, u32[]{:S(2)}) copy-start(bf16[512,2048]{1,0:T(8,128)(2,1)} %param.20) | copy-start | bytes 6291460
  7.2 5.9 copy-start.4
  7.2 60.7 %all-gather.5.cloned.1.call-start = ((), (), s32[]{:S(2)}) async-start(), calls=%async_computation.10 | async-start | bytes 1179648 | tf_op jit(solution)/shard_map/all_gather | solution.py:105
  10.2 9.7 copy-start.40
  13.1 1.3 copy-start.25
  13.1 2.7 copy-start.43
  13.4 1.0 copy-start.7
  19.8 95.5 %all-gather.3.cloned.1.call-start = ((), (), s32[]{:S(2)}) async-start(), calls=%async_computation.9 | async-start | bytes 1179648 | tf_op jit(solution)/shard_map/all_gather | solution.py:106
  19.9 1.7 copy-start.21
  22.7 161.9 %all-reduce.6.cloned.1.call-start = ((), (), s32[]{:S(2)}) async-start(), calls=%async_computation.11 | async-start | bytes 4194304 | tf_op jit(solution)/shard_map/psum | solution.py:127
  26.7 2.7 copy-start.48
  29.4 1.7 copy-start.42
  70.3 2.0 copy-start.2
  128.3 118.1 %all-reduce.8.cloned.1.call-start = ((), (), s32[]{:S(2)}) async-start(), calls=%async_computation.12 | async-start | bytes 2097152 | tf_op jit(solution)/shard_map/psum | solution.py:148
  184.6 2.2 copy-start.10
  186.8 7.0 slice-start
  188.7 5.1 copy-start.11
  188.7 5.1 slice-start.1
  188.7 7.0 slice-start.4
  193.9 1.9 copy-start.23
  193.9 1.9 slice-start.5
  193.9 7.1 slice-start.2
  195.8 5.2 slice-start.3
  199.2 1.8 copy-start.34
  199.2 1.8 copy-start.36
  203.9 225.1 %reduce-scatter.14.cloned.1.call-start = ((), (), s32[]{:S(2)}) async-start(), calls=%async_computation.13 | async-start | bytes 1179648 | tf_op jit(solution)/shard_map/reduce_scatter | solution.py:192
  246.4 2.5 copy-start.9
  246.5 2.8 copy-start.14
  251.1 1.4 copy-start.5
  258.9 1.7 copy-start.26
  260.3 226.7 %reduce-scatter.28.cloned.1.call-start = ((), (), s32[]{:S(2)}) async-start(), calls=%async_computation.20 | async-start | bytes 1179648
  260.6 3.5 copy-start.3
  264.1 1.0 copy-start.28
  413.9 163.3 %all-reduce.10.cloned.1.call-start = ((), (), s32[]{:S(2)}) async-start(), calls=%async_computation.22 | async-start | bytes 4194304 | tf_op jit(solution)/shard_map/psum | solution.py:137
  414.8 5.9 copy-start.20
  422.4 3.7 copy-start.19
  423.8 5.2 copy-start.22
  506.8 8.6 copy-start.44
  515.4 3.3 copy-start.17
  516.1 2.7 copy-start.16
  516.1 2.7 copy-start.31
  520.5 1.2 copy-start.8
  520.5 1.2 copy-start.39
  520.5 2.8 copy-start.32
  520.5 246.0 %reduce-scatter.20.cloned.1.call-start = ((), (), s32[]{:S(2)}) async-start(), calls=%async_computation.16 | async-start | bytes 1081344 | tf_op jit(solution)/shard_map/reduce_scatter | solution.py:246
  523.3 428.7 %reduce-scatter.16.cloned.1.call-start = ((), (), s32[]{:S(2)}) async-start(), calls=%async_computation.14 | async-start | bytes 2162688 | tf_op jit(solution)/shard_map/reduce_scatter | solution.py:240
  525.5 3.0 copy-start.6
  525.5 3.0 copy-start.29
  525.5 609.4 %reduce-scatter.18.cloned.1.call-start = ((), (), s32[]{:S(2)}) async-start(), calls=%async_computation.15 | async-start | bytes 1081344 | tf_op jit(solution)/shard_map/reduce_scatter | solution.py:243
  528.4 792.3 %reduce-scatter.22.cloned.1.call-start = ((), (), s32[]{:S(2)}) async-start(), calls=%async_computation.17 | async-start | bytes 2162688 | tf_op jit(solution)/shard_map/reduce_scatter | solution.py:249
  530.6 1.2 copy-start.24
  530.6 1.4 copy-start.33
  530.6 1021.3 %reduce-scatter.30.cloned.1.call-start = ((), (), s32[]{:S(2)}) async-start(), calls=%async_computation.21 | async-start | bytes 6488064
  545.2 1.2 copy-start.12
  545.2 1.5 copy-start.37
  545.2 1240.7 %reduce-scatter.26.cloned.1.call-start = ((), (), s32[]{:S(2)}) async-start(), calls=%async_computation.19 | async-start | bytes 6488064 | tf_op jit(solution)/shard_map/reduce_scatter | solution.py:255
  551.1 1.1 copy-start.35
  551.1 1468.3 %reduce-scatter.24.cloned.1.call-start = ((), (), s32[]{:S(2)}) async-start(), calls=%async_computation.18 | async-start | bytes 6488064 | tf_op jit(solution)/shard_map/reduce_scatter | solution.py:252
  556.7 1.3 copy-start.15
  577.2 560.4 %copy-start.46 = (f32[128]{0:T(128)S(1)}, f32[128]{0:T(128)}, u32[]{:S(2)}) copy-start(f32[128]{0:T(128)} %get-tuple-element.52) | copy-start | bytes 1540
  577.2 560.4 %copy-start.47 = (f32[128]{0:T(128)S(1)}, f32[128]{0:T(128)}, u32[]{:S(2)}) copy-start(f32[128]{0:T(128)} %get-tuple-element.54) | copy-start | bytes 1540
  577.2 625.5 %copy-start.13 = (bf16[256,2048]{1,0:T(8,128)(2,1)S(1)}, bf16[256,2048]{1,0:T(8,128)(2,1)}, u32[]{:S(2)}) copy-start(bf16[256,2048]{1,0:T(8,128)(2,1)} %get-tuple-element.61) | copy-start | bytes 3145732
  577.2 625.5 %copy-start.41 = (f32[256]{0:T(256)S(1)}, f32[256]{0:T(256)}, u32[]{:S(2)}) copy-start(f32[256]{0:T(256)} %copy-done.40) | copy-start | bytes 3076
  1322.2 698.9 %copy-start.1 = (bf16[512,2048]{1,0:T(8,128)(2,1)S(1)}, bf16[512,2048]{1,0:T(8,128)(2,1)}, u32[]{:S(2)}) copy-start(bf16[512,2048]{1,0:T(8,128)(2,1)} %param.20) | copy-start | bytes 6291460
  (5 other events, 3.8 us)
Sparse Core Ops, SparseCore 0:
  19.9 47.8 all-gather.4
  70.8 44.5 all-gather.2
  128.5 56.1 all-reduce.5
  204.0 42.3 all-reduce.7
  260.4 72.8 reduce-scatter.13
  414.1 72.8 reduce-scatter.27
  520.6 56.5 all-reduce.9
  579.7 186.8 reduce-scatter.19
  768.9 182.9 reduce-scatter.15
  954.3 180.6 reduce-scatter.17
  1137.3 183.3 reduce-scatter.21
  1326.5 225.4 reduce-scatter.29
  1557.8 227.9 reduce-scatter.25
  1791.6 227.7 reduce-scatter.23
where the time goes:
time: 2040 us; the launch traced here: 2030 us
  waiting for transfers between devices  1600 us (78%)
  local copies, waits for them, and re-layouts  227 us (11%)
  matrix products  74.4 us (4%)
  blocking collectives  65.1 us (3%)
  other arithmetic  45 us (2%)
    unnamed x16, waiting for transfers between devices  280 us
    reduce_scatter x1, waiting for transfers between devices, local(): lax.psum_scatter(gate_grad.astype(jnp.bfloat16), ('dp', 'context'), scatt...  232 us
    reduce_scatter x1, waiting for transfers between devices, local(): lax.psum_scatter(up_grad.astype(jnp.bfloat16), ('dp', 'context'), scatter...  232 us
    unnamed x117, local copies, waits for them, and re-layouts  200 us
    reduce_scatter x1, waiting for transfers between devices, local(): lax.psum_scatter(value_grad.astype(jnp.bfloat16), ('dp', 'context'), scat...  186 us
    reduce_scatter x1, waiting for transfers between devices, local(): lax.psum_scatter(query_grad.astype(jnp.bfloat16), ('dp', 'context'), scat...  184 us
    reduce_scatter x1, waiting for transfers between devices, local(): lax.psum_scatter(key_grad.astype(jnp.bfloat16), ('dp', 'context'), scatte...  182 us
    reduce_scatter x1, waiting for transfers between devices, local(): lax.psum_scatter(out_weight_grad.astype(jnp.bfloat16), ('dp', 'context'),...  117 us
  transfers between devices with their start and end apart: 14, of which 13 were waited for; matrix products, arithmetic and copies ran while one was open for 12% of the time, Pallas kernels for 0%

commit v1 on v0

--- a/solution.py
+++ b/solution.py
@@ -1,7 +1,117 @@
 import jax
 import jax.numpy as jnp
 from jax import lax
+from jax.experimental import pallas as pl
+from jax.experimental.pallas import tpu as pltpu
 from jax.sharding import PartitionSpec as P
+
+MESH = pl.DeviceIdType.MESH
+BF=jnp.bfloat16; F32=jnp.float32
+ORDERS=(("y0","z0","y1","z1","xh"),("z0","y1","z1","y0","xh"),("y1","z1","y0","z0","xh"),("z1","y0","z0","y1","xh"))
+
+def me_place():
+    c=lax.axis_index("context")
+    return (lax.axis_index("dp"), c//2, c%2, lax.axis_index("tensor"))
+def flip4(v, which):
+    return v+1-2*(v%2) if which=="0" else 3-v
+def partner(place, dim):
+    y,z,h,t=place
+    if dim=="xh": return (y,z,1-h,t)
+    if dim[0]=="y": return (flip4(y,dim[1]),z,h,t)
+    return (y,flip4(z,dim[1]),h,t)
+def dev(place):
+    y,z,h,t=place
+    return (y,z*2+h,t)
+def runs(base, remaining):
+    y,z,h,_=base
+    def ring(v,a):
+        both=(a+"0" in remaining, a+"1" in remaining)
+        if all(both): return None
+        if both[0]: return [v,flip4(v,"0")]
+        if both[1]: return [v,flip4(v,"1")]
+        return [v]
+    ys=ring(y,"y"); zs=ring(z,"z")
+    ys=[0,1,2,3] if ys is None else ys
+    out=[]
+    for yy in ys:
+        if zs is None:
+            out.append((yy*512,512))
+        else:
+            for zz in zs:
+                if "xh" in remaining: out.append((yy*512+zz*128,128))
+                else: out.append((yy*512+zz*128+h*64,64))
+    return out
+
+def send_step(acc, recv, ssem, rsem, b, k, s, me):
+    dim=ORDERS[k][s]; rem=ORDERS[k][s+1:]
+    p=partner(me,dim); off=0
+    for row,n in runs(p,rem):
+        pltpu.make_async_remote_copy(src_ref=acc.at[b,k,pl.ds(pl.multiple_of(row,64),n)],dst_ref=recv[s].at[b,k,pl.ds(off,n)],
+            send_sem=ssem.at[b,k,s],recv_sem=rsem.at[b,k,s],device_id=dev(p),device_id_type=MESH).start()
+        off+=n
+def add_step(acc, recv, ssem, rsem, b, k, s, me, out=None):
+    rem=ORDERS[k][s+1:]
+    pltpu.make_async_copy(recv[s].at[b,k],recv[s].at[b,k],rsem.at[b,k,s]).wait()
+    off=0
+    for row,n in runs(me,rem):
+        step=min(n,128)
+        def body(i,_,row=row,off=off,step=step):
+            r=pl.ds(pl.multiple_of(row+i*step,64),step)
+            v=acc[b,k,r].astype(F32)+recv[s][b,k,pl.ds(pl.multiple_of(off+i*step,64),step)].astype(F32)
+            if out is None: acc[b,k,r]=v.astype(BF)
+            else: out[b,:,k*384:(k+1)*384]=v
+            return 0
+        if n//step==1: body(0,0)
+        else: lax.fori_loop(0,n//step,body,0)
+        off+=n
+def wait_send(acc,recv,ssem,b,k,s):
+    pltpu.make_async_copy(recv[s].at[b,k],recv[s].at[b,k],ssem.at[b,k,s]).wait()
+
+def rs_kernel(*refs):
+    ins=refs[:7]; out=refs[7]; acc,r1,r2,r3,r4,r5,lsem,ssem,rsem=refs[8:]
+    recv=(r1,r2,r3,r4,r5)
+    me=me_place()
+    bar=pltpu.get_barrier_semaphore()
+    for d in ORDERS[0]:
+        pl.semaphore_signal(bar,inc=1,device_id=dev(partner(me,d)),device_id_type=MESH)
+    pieces=[]
+    for b in range(3):
+        for k in range(4):
+            pieces.append((b,k,0,ins[b],k*384,384))
+    col=0
+    for r in ins[3:]:
+        w=r.shape[1]; c=0
+        while c<w:
+            k=(col+c)//384; o=(col+c)%384; n=min(384-o,w-c)
+            pieces.append((3,k,o,r,c,n)); c+=n
+        col+=w
+    cps={}
+    for b,k,o,r,c,n in pieces:
+        cp=pltpu.make_async_copy(r.at[:,c:c+n],acc.at[b,k,:,o:o+n],lsem.at[len(cps)])
+        cp.start(); cps[(b,k,o)]=cp
+    pl.semaphore_wait(bar,5)
+    for b in range(4):
+        for key,cp in cps.items():
+            if key[0]==b: cp.wait()
+        for k in range(4): send_step(acc,recv,ssem,rsem,b,k,0,me)
+    for w in range(4+4):
+        for b in range(4):
+            s=w-b
+            if 0<=s<5:
+                for k in range(4):
+                    add_step(acc,recv,ssem,rsem,b,k,s,me,out if s==4 else None)
+                    if s<4: send_step(acc,recv,ssem,rsem,b,k,s+1,me)
+    for b in range(4):
+        for k in range(4):
+            for s in range(5): wait_send(acc,recv,ssem,b,k,s)
+
+def reduce_weights(parts):
+    npieces=12+sum(1 for _ in range(6))
+    return pl.pallas_call(rs_kernel,out_shape=jax.ShapeDtypeStruct((4,64,1536),F32),
+      in_specs=[pl.BlockSpec(memory_space=pl.ANY)]*7,out_specs=pl.BlockSpec(memory_space=pltpu.VMEM),
+      scratch_shapes=[pltpu.VMEM((4,4,2048,384),BF)]+[pltpu.VMEM((4,4,1024>>s,384),BF) for s in range(5)]+
+        [pltpu.SemaphoreType.DMA((24,)),pltpu.SemaphoreType.DMA((4,4,5)),pltpu.SemaphoreType.DMA((4,4,5))],
+      compiler_params=pltpu.CompilerParams(collective_id=1,has_side_effects=True,vmem_limit_bytes=62*2**20))(*parts)
 
 EPSILON = 1e-06
 ROPE_BASE = 1000000.0
@@ -236,29 +346,13 @@
     gain_grads = lax.psum(
         (gain_one_term, query_gain_term, key_gain_term, gain_two_term), ("dp", "context", "tensor")
     )
-    query_part, key_part, value_part, out_part, gate_part, up_part, down_part = (
-        lax.psum_scatter(
-            query_grad.astype(jnp.bfloat16), ("dp", "context"), scatter_dimension=0, tiled=True
-        ).astype(jnp.float32),
-        lax.psum_scatter(
-            key_grad.astype(jnp.bfloat16), ("dp", "context"), scatter_dimension=0, tiled=True
-        ).astype(jnp.float32),
-        lax.psum_scatter(
-            value_grad.astype(jnp.bfloat16), ("dp", "context"), scatter_dimension=0, tiled=True
-        ).astype(jnp.float32),
-        lax.psum_scatter(
-            out_weight_grad.astype(jnp.bfloat16), ("dp", "context"), scatter_dimension=0, tiled=True
-        ).astype(jnp.float32),
-        lax.psum_scatter(
-            gate_grad.astype(jnp.bfloat16), ("dp", "context"), scatter_dimension=0, tiled=True
-        ).astype(jnp.float32),
-        lax.psum_scatter(
-            up_grad.astype(jnp.bfloat16), ("dp", "context"), scatter_dimension=0, tiled=True
-        ).astype(jnp.float32),
-        lax.psum_scatter(
-            down_grad.astype(jnp.bfloat16), ("dp", "context"), scatter_dimension=0, tiled=True
-        ).astype(jnp.float32),
-    )
+    low = lambda v: v.astype(jnp.bfloat16)
+    summed = reduce_weights(
+        (low(down_grad), low(gate_grad), low(up_grad), low(out_weight_grad), low(query_grad), low(key_grad), low(value_grad))
+    )
+    down_part, gate_part, up_part = summed[0], summed[1], summed[2]
+    out_part, query_part = summed[3, :, :512], summed[3, :, 512:1024]
+    key_part, value_part = summed[3, :, 1024:1280], summed[3, :, 1280:]
     return (
         block_out,
         tokens_grad,

time: 2040 us -> 810 us (0.40)
  waiting for transfers between devices: 1600 us -> 253 us
  Pallas kernels: 0 us -> 144 us
    reduce_scatter x6 -> x0, waiting for transfers between devices: 1130 us -> none  [the longest x1 232 us: local(): lax.psum_scatter(gate_grad.astype(jnp.bfloat16), ('dp', 'context'), scatt...]
    unnamed x16 -> x8, waiting for transfers between devices: 280 us -> 37.6 us
    pallas_call x0 -> x1, Pallas kernels: none -> 144 us  [reduce_weights(): pl.pallas_call(rs_kernel, out_shape=jax.ShapeDtypeStruct((4, 64, 1536), F...]
    reduce_scatter x1, waiting for transfers between devices: 0.01 us -> 40.2 us  [local(): lax.psum_scatter(grad_value_full.reshape(sequences, length, kv_local * he...]
    unnamed x117 -> x142, local copies, waits for them, and re-layouts: 200 us -> 183 us
  transfers between devices with their start and end apart: 14 -> 7, of which waited for: 13 -> 6; matrix products, arithmetic and copies ran while one was open for 12% -> 12% of each run, Pallas kernels for 0% -> 18%
where the time goes in v1:
time: 810 us; the launch traced here: 800 us
  waiting for transfers between devices  253 us (31%)
  local copies, waits for them, and re-layouts  214 us (26%)
  Pallas kernels  144 us (18%)
  matrix products  74.7 us (9%)
  blocking collectives  63.9 us (8%)
  other arithmetic  33.1 us (4%)
  between operations  15.2 us (2%)
    unnamed x142, local copies, waits for them, and re-layouts  183 us
    pallas_call x1, Pallas kernels, reduce_weights(): pl.pallas_call(rs_kernel, out_shape=jax.ShapeDtypeStruct((4, 64, 1536), F...  144 us
    psum x1, blocking collectives, local(): lax.psum((gain_one_term, query_gain_term, key_gain_term, gain_two_term),...  63.9 us
    psum x1, waiting for transfers between devices, local(): attention_out = lax.psum(matmul(mixture, w_out), 'tensor')  55.6 us
    all_gather x1, waiting for transfers between devices, local(): lax.all_gather(value_local, 'context', axis=1, tiled=True)  42.6 us
    reduce_scatter x1, waiting for transfers between devices, local(): lax.psum_scatter(grad_value_full.reshape(sequences, length, kv_local * he...  40.2 us
    psum x1, waiting for transfers between devices, local(): lax.psum((matmul_nt(grad_gate, w_gate) + matmul_nt(grad_up, w_up)).astype...  40.1 us
    unnamed x8, waiting for transfers between devices  37.6 us
  transfers between devices with their start and end apart: 7, of which 6 were waited for; matrix products, arithmetic and copies ran while one was open for 12% of the time, Pallas kernels for 18%

profile of v1, /device:TPU:0, one launch (start us, length us, event | category | flops | bytes accessed | tf_op | source)
XLA Modules:
  0.0 800.2 jit_solution(14627185182962957667)
XLA Ops:
  8.1 1.5 fusion.13
  9.6 2.3 copy.101
  16.5 1.6 convert_element_type.198
  18.1 1.6 copy.68
  19.7 1.7 bitcast_multiply_fusion.2
  22.6 4.0 copy.104
  26.5 2.4 multiply_reduce_fusion.5
  30.5 37.2 %all-gather.5.cloned.1.call-done = bf16[2,1024,256]{1,2,0:T(8,128)(2,1)} async-done(((bf16[2,128,256]{1,2,0:T(8,128)(2,1)}), bf16[2,1024,256]{1,2,0:T(8,128)(2,1)}) %all-gather.5.cloned.1.call-update) | async-done | bytes 1048592 | tf_op jit(solution)/shard_map/all_gather | solution.py:215
  67.7 2.2 fusion.33
  70.0 2.0 copy-done.1
  72.6 42.6 %all-gather.3.cloned.1.call-done = bf16[2,1024,256]{2,1,0:T(8,128)(2,1)} async-done(((bf16[2,128,256]{2,1,0:T(8,128)(2,1)}), bf16[2,1024,256]{2,1,0:T(8,128)(2,1)}) %all-gather.3.cloned.1.call-update) | async-done | bytes 1048592 | tf_op jit(solution)/shard_map/all_gather | solution.py:216
  115.2 1.5 copy.66
  116.7 4.1 fusion.23
  120.9 1.8 copy.74
  123.7 3.7 fusion.34
  128.2 55.6 %all-reduce.6.cloned.1.call-done = f32[256,2048]{1,0:T(8,128)} async-done(((f32[256,2048]{1,0:T(8,128)}), f32[256,2048]{1,0:T(8,128)}) %all-reduce.6.cloned.1.call-update) | async-done | bytes 2097168 | tf_op jit(solution)/shard_map/psum | solution.py:237
  183.8 2.1 multiply_reduce_fusion.2
  186.0 2.0 multiply_convert_fusion
  188.0 5.0 fusion.35
  193.1 1.8 fusion.36
  195.0 3.3 multiply_convert_fusion.2
  198.4 1.8 fusion.37
  200.3 2.8 fusion.8
  205.6 40.1 %all-reduce.8.cloned.1.call-done = bf16[256,2048]{1,0:T(8,128)(2,1)} async-done(((bf16[256,2048]{1,0:T(8,128)(2,1)}), bf16[256,2048]{1,0:T(8,128)(2,1)}) %all-reduce.8.cloned.1.call-update) | async-done | bytes 1048592 | tf_op jit(solution)/shard_map/psum | solution.py:258
  245.7 1.7 multiply_reduce_fusion.1
  247.8 2.0 multiply_add_fusion
  249.9 1.5 convolution_convert_fusion.7
  251.4 1.7 reshape.299
  253.1 1.8 copy.83
  254.9 3.8 fusion.1
  259.6 1.3 copy-done.11
  260.9 1.9 fusion.12
  262.8 49.5 %copy.109 = bf16[2,1024,256]{0,2,1:T(8,128)(2,1)} copy(bf16[2,1024,256]{1,2,0:T(8,128)(2,1)} %bitcast.179) | data formatting | bytes 2097152
  312.3 97.3 %reshape.315 = bf16[1024,512]{1,0:T(8,128)(2,1)} reshape(bf16[1024,256,2]{2,1,0:T(8,128)(2,1)} %bitcast.47) | data formatting | bytes 2097152
  410.2 6.1 convolution_convert_fusion.refs_2_
  416.3 4.5 convolution_convert_fusion.1.refs_1_
  420.8 4.6 fusion.refs_0_
  425.4 2.8 convolution_convert_fusion.6
  428.2 1.8 bitcast_convert_fusion
  430.0 2.3 copy.85
  432.3 3.6 fusion.21
  436.0 2.0 copy.79
  438.0 2.3 reshape.300
  440.3 1.5 convert_element_type.214
  441.8 1.7 fusion.24
  445.1 37.5 %reduce-scatter.7.cloned.1.call-done = bf16[128,512]{1,0:T(8,128)(2,1)} async-done(((bf16[1024,512]{1,0:T(8,128)(2,1)}), bf16[128,512]{1,0:T(8,128)(2,1)}) %reduce-scatter.7.cloned.1.call-update) | async-done | bytes 131088
  482.6 20.0 %reshape.316 = bf16[128,256,2]{2,1,0:T(8,128)(2,1)} reshape(bf16[128,512]{1,0:T(8,128)(2,1)} %reduce-scatter.7.cloned.1.call-done) | data formatting | bytes 262144
  502.6 9.1 %copy.110 = bf16[2,128,256]{1,0,2:T(2,128)(2,1)} copy(bf16[2,128,256]{0,2,1:T(8,128)(2,1)} %bitcast.173) | data formatting | bytes 262144
  511.7 1.7 reshape.306
  515.3 1.8 fusion.38
  517.1 40.2 %reduce-scatter.5.cloned.1.call-done = bf16[2,128,256]{2,1,0:T(8,128)(2,1)} async-done(((bf16[2,1024,256]{2,1,0:T(8,128)(2,1)}), bf16[2,128,256]{2,1,0:T(8,128)(2,1)}) %reduce-scatter.5.cloned.1.call-update) | async-done | bytes 131088 | tf_op jit(solution)/shard_map/reduce_scatter | solution.py:302
  557.3 1.5 fusion.39
  559.0 3.4 fusion.7
  562.5 3.4 convolution_convert_fusion.3.refs_4_
  565.8 2.1 convolution_convert_fusion.4.refs_3_
  567.9 1.4 convolution_convert_fusion.5.refs_5_
  569.4 1.5 fusion.9.refs_6_
  570.9 144.3 %shard_map.228 = f32[4,64,1536]{2,1,0:T(8,128)} custom-call(bf16[2048,1536]{1,0:T(8,128)(2,1)} %fusion.refs_0_, bf16[2048,1536]{1,0:T(8,128)(2,1)} %convolution_convert_fusion.1.refs_1_, bf16[2048,1536]{1,0:T(8,128)(2,1)} %convolution_convert_fusion.refs_2_, bf16[2048,512]{1,0:T(8,128)(2,1)} %convolution_convert_fusion.4.refs_3_, ...), custom_call_target="tpu_custom_call" | custom-call | tf_op jit(solution)/shard_map/pallas_call | solution.py:110
  715.2 1.5 slice_bitcast_fusion.5
  716.8 1.7 slice_bitcast_fusion.3
  718.4 2.3 slice_bitcast_fusion
  720.7 1.6 convert_element_type.231
  724.3 63.9 %all-reduce = (f32[2048]{0:T(1024)}, f32[128]{0:T(128)}, f32[128]{0:T(128)}, f32[2048]{0:T(1024)}) all-reduce(f32[2048]{0:T(1024)S(1)} %fusion.25, f32[128]{0:T(128)S(1)} %copy-done.57, f32[128]{0:T(128)S(1)} %copy-done.58, f32[2048]{0:T(1024)S(1)} %copy-done.47), channel_id=1, replica_groups=mesh['dp'=4,'context'=8,'tensor'=4] {'dp','context','tensor'}, use_global_device_ids=true, to_apply=%region_18.19 | all-reduce | flops 4352 | bytes 34816 | tf_op jit(solution)/shard_map/psum | solution.py:346
  788.2 5.0 add_convert_fusion
  (200 shorter events, 20.6 us)
Async XLA Ops:
  7.2 14.2 %copy-start = (bf16[2048,256]{1,0:T(8,128)(2,1)S(1)}, bf16[2048,256]{1,0:T(8,128)(2,1)}, u32[]{:S(2)}) copy-start(bf16[2048,256]{1,0:T(8,128)(2,1)} %param.17) | copy-start | bytes 3145732
  7.2 4.7 copy-start.4
  7.2 60.5 %all-gather.5.cloned.1.call-start = ((), (), s32[]{:S(2)}) async-start(), calls=%async_computation.3 | async-start | bytes 1179648 | tf_op jit(solution)/shard_map/all_gather | solution.py:215
  9.6 10.1 %copy-start.48 = (f32[256]{0:T(256)}, f32[256]{0:T(256)S(1)}, u32[]{:S(2)}) copy-start(f32[256]{0:T(256)S(1)} %get-tuple-element.50) | copy-start | bytes 3076
  11.9 1.7 copy-start.59
  12.2 14.3 %copy-start.7 = (bf16[2,128,2048]{2,1,0:T(8,128)(2,1)}, bf16[2,128,2048]{2,1,0:T(8,128)(2,1)S(1)}, u32[]{:S(2)}) copy-start(bf16[2,128,2048]{2,1,0:T(8,128)(2,1)S(1)} %fusion.15) | copy-start | bytes 3145732
  13.6 7.8 copy-start.45
  19.7 95.5 %all-gather.3.cloned.1.call-start = ((), (), s32[]{:S(2)}) async-start(), calls=%async_computation.2 | async-start | bytes 1179648 | tf_op jit(solution)/shard_map/all_gather | solution.py:216
  22.5 161.3 %all-reduce.6.cloned.1.call-start = ((), (), s32[]{:S(2)}) async-start(), calls=%async_computation.4 | async-start | bytes 4194304 | tf_op jit(solution)/shard_map/psum | solution.py:237
  26.5 2.4 copy-start.60
  30.1 39.8 %copy-start.26 = (bf16[2,128,2,2,64]{4,1,3,2,0:T(8,128)(2,1)}, bf16[2,128,2,2,64]{4,1,3,2,0:T(8,128)(2,1)S(1)}, u32[]{:S(2)}) copy-start(bf16[2,128,2,2,64]{4,1,3,2,0:T(8,128)(2,1)S(1)} %copy.70) | copy-start | bytes 393220
  30.4 39.6 %copy-start.28 = (bf16[2,128,2,2,64]{4,1,3,2,0:T(8,128)(2,1)}, bf16[2,128,2,2,64]{4,1,3,2,0:T(8,128)(2,1)S(1)}, u32[]{:S(2)}) copy-start(bf16[2,128,2,2,64]{4,1,3,2,0:T(8,128)(2,1)S(1)} %copy.71) | copy-start | bytes 393220
  70.0 2.0 copy-start.1
  70.0 46.7 %copy-start.44 = (f32[2,2,2,128]{3,2,1,0:T(2,128)}, f32[2,2,2,128]{3,2,1,0:T(2,128)S(1)}, u32[]{:S(2)}) copy-start(f32[2,2,2,128]{3,2,1,0:T(2,128)S(1)} %get-tuple-element.55) | copy-start | bytes 12292
  72.6 48.3 %copy-start.50 = (f32[2,2,2,128]{3,2,1,0:T(2,128)}, f32[2,2,2,128]{3,2,1,0:T(2,128)S(1)}, u32[]{:S(2)}) copy-start(f32[2,2,2,128]{3,2,1,0:T(2,128)S(1)} %fusion.4) | copy-start | bytes 12292
  116.7 4.1 copy-start.25
  123.7 3.8 copy-start.30
  127.5 118.2 %all-reduce.8.cloned.1.call-start = ((), (), s32[]{:S(2)}) async-start(), calls=%async_computation.5 | async-start | bytes 2097152 | tf_op jit(solution)/shard_map/psum | solution.py:258
  183.8 2.2 copy-start.12
  186.0 2.0 copy-start.51
  186.0 7.0 slice-start.2
  188.0 5.0 copy-start.13
  188.0 5.0 slice-start.3
  188.0 6.9 slice-start.4
  193.1 1.9 copy-start.22
  193.1 1.9 slice-start.5
  193.1 5.3 slice-start
  195.0 3.4 slice-start.1
  198.4 1.8 copy-start.36
  198.4 1.9 copy-start.38
  200.2 45.4 %copy-start.9 = (f32[256,2048]{1,0:T(8,128)S(1)}, f32[256,2048]{1,0:T(8,128)}, u32[]{:S(2)}) copy-start(f32[256,2048]{1,0:T(8,128)} %get-tuple-element.24) | copy-start | bytes 6291460
  203.1 279.5 %reduce-scatter.7.cloned.1.call-start = ((), (), s32[]{:S(2)}) async-start(), calls=%async_computation.7 | async-start | bytes 1179648
  245.7 1.9 copy-start.10
  245.7 2.2 copy-start.16
  245.7 2.2 copy-start.52
  247.8 2.0 copy-start.17
  249.8 316.0 %copy-start.6 = (f32[256,2048]{1,0:T(8,128)}, f32[256,2048]{1,0:T(8,128)S(1)}, u32[]{:S(2)}) copy-start(f32[256,2048]{1,0:T(8,128)S(1)} %multiply_add_fusion) | copy-start | bytes 6291460
  249.8 5.0 copy-start.41
  254.9 3.8 copy-start.2
  258.7 2.2 copy-start.27
  258.7 2.2 copy-start.29
  409.6 147.7 %reduce-scatter.5.cloned.1.call-start = ((), (), s32[]{:S(2)}) async-start(), calls=%async_computation.6 | async-start | bytes 1179648 | tf_op jit(solution)/shard_map/reduce_scatter | solution.py:302
  410.1 6.2 copy-start.14
  410.1 6.2 copy-start.37
  410.2 15.2 %slice-start.6 = ((s8[6291456]{0:T(1024)(128)(4,1)}), s8[4194304]{0:T(1024)(128)(4,1)S(1)}, s32[]{:S(2)}) async-start(s8[6291456]{0:T(1024)(128)(4,1)} %bitcast.207), calls=%async_computation.15 | async-start | bytes 8388608
  416.3 4.5 copy-start.23
  416.3 4.5 copy-start.35
  416.3 9.1 %slice-start.7 = ((s8[6291456]{0:T(1024)(128)(4,1)}), s8[2097152]{0:T(1024)(128)(4,1)S(1)}, s32[]{:S(2)}) async-start(s8[6291456]{0:T(1024)(128)(4,1)} %bitcast.207), calls=%async_computation.16 | async-start | bytes 4194304
  425.4 2.8 copy-start.3
  425.4 2.8 copy-start.32
  432.3 288.4 %all-reduce.10.cloned.1.call-start = ((), (), s32[]{:S(2)}) async-start(), calls=%async_computation.8 | async-start | bytes 4194304 | tf_op jit(solution)/shard_map/psum | solution.py:247
  440.2 3.3 copy-start.34
  440.2 3.3 copy-start.20
  440.2 3.4 copy-start.43
  440.2 3.4 copy-start.54
  502.6 11.8 %copy-start.46 = (f32[256,2]{0,1:T(2,128)S(1)}, f32[256,2]{0,1:T(2,128)}, u32[]{:S(2)}) copy-start(f32[256,2]{0,1:T(2,128)} %copy-done.45) | copy-start | bytes 6148
  502.6 11.8 %copy-start.55 = (f32[128]{0:T(128)S(1)}, f32[128]{0:T(128)}, u32[]{:S(2)}) copy-start(f32[128]{0:T(128)} %convert_element_type.195) | copy-start | bytes 1540
  513.4 1.9 copy-start.21
  517.1 41.8 %copy-start.33 = (bf16[256,4,128]{0,2,1:T(8,128)(2,1)S(1)}, bf16[256,4,128]{0,2,1:T(8,128)(2,1)}, u32[]{:S(2)}) copy-start(bf16[256,4,128]{0,2,1:T(8,128)(2,1)} %multiply_convert_fusion.5) | copy-start | bytes 786436
  562.4 3.4 copy-start.31
  565.8 2.1 copy-start.8
  720.7 1.9 copy-start.15
  722.6 1.7 copy-start.57
  722.6 1.7 copy-start.58
  (12 other events, 14.3 us)
Sparse Core Ops, SparseCore 0:
  19.8 47.8 all-gather.4
  70.6 44.5 all-gather.2
  127.6 56.1 all-reduce.5
  203.2 42.3 all-reduce.7
  409.7 72.8 reduce-scatter.6
  486.5 70.7 reduce-scatter.4
  562.6 56.5 all-reduce.9
